TPU v7x, 128 devices: a whole 4x4x4 slice. The times are simulated.
128 devices in a mesh: rep: 4 (over y_lo, core), fsdp: 32 (over y_hi, x, z).
Axes of the slice: x: 4, y: 4 (y_hi: 2, y_lo: 2; y = y_hi * 2 + y_lo), z: 4, core: 2. Of those that a mesh axis runs over, the one named last changes fastest.
Arguments:
- tokens: bfloat16 [2, 128, 128, 1024], P(None, ('rep', 'fsdp')), may hold values from -6 to 6
- segments: int32 [2, 128, 128], P(None, ('rep', 'fsdp')), may hold values from 0 to 31, never falling along the last dimension, each value on 1 to 64 neighbouring positions
- routes: int32 [2, 128, 128, 8], P(None, ('rep', 'fsdp')), may hold values from 0 to 31, all different within a row; in each aligned block of 128 rows (0 to 127, 128 to 255, ..., all dimensions but the last counted through in order) at most 48 rows name the same one
- cotangent: bfloat16 [2, 128, 128, 1024], P(None, ('rep', 'fsdp')), may hold values from -6 to 6
- attn_gain: bfloat16 [1024], P('fsdp'), may hold values from 0.5 to 1.5
- moe_gain: bfloat16 [1024], P('fsdp'), may hold values from 0.5 to 1.5
- w_query: bfloat16 [1024, 1024], P('fsdp'), may hold values from -0.75 to 0.75
- w_key: bfloat16 [1024, 512], P('fsdp'), may hold values from -0.75 to 0.75
- w_value: bfloat16 [1024, 512], P('fsdp'), may hold values from -0.1875 to 0.1875
- w_output: bfloat16 [1024, 1024], P('fsdp'), may hold values from -1.5 to 1.5
- w_router: bfloat16 [1024, 32], P('fsdp'), may hold values from -0.09375 to 0.09375
- w_gate: bfloat16 [32, 1024, 512], P('fsdp'), may hold values from -0.1875 to 0.1875
- w_up: bfloat16 [32, 1024, 512], P('fsdp'), may hold values from -0.1875 to 0.1875
- w_down: bfloat16 [32, 512, 1024], P('fsdp'), may hold values from -6 to 6
Outputs:
- output: bfloat16 [2, 128, 128, 1024], P(None, ('rep', 'fsdp'))
- grad_tokens: float32 [2, 128, 128, 1024], P(None, ('rep', 'fsdp'))
- grad_attn_gain: float32 [1024], P('fsdp')
- grad_moe_gain: float32 [1024], P('fsdp')
- grad_query: float32 [1024, 1024], P('fsdp')
- grad_key: float32 [1024, 512], P('fsdp')
- grad_value: float32 [1024, 512], P('fsdp')
- grad_w_output: float32 [1024, 1024], P('fsdp')
- grad_router: float32 [1024, 32], P('fsdp')
- grad_gate: float32 [32, 1024, 512], P('fsdp')
- grad_up: float32 [32, 1024, 512], P('fsdp')
- grad_down: float32 [32, 512, 1024], P('fsdp')
Inputs may be any that keep to these rules, and one draw needn't show every extreme that they name: `segments`: within a sequence segment numbers never fall; every segment has 1 to 64 tokens and some segment has exactly 64. `routes`: A token's 8 experts differ. Within one sequence no expert is named by more than 48 tokens, and in every draw some sequence names some expert exactly 48 times.
All inputs are finite; a program needn't handle non-finite values.
Results may differ from a plain program's by a relative error of at most 0.018.
Values may be sent and summed in bfloat16 or wider, within the bound.
A program may use at most 192 MiB of HBM per device.

v0:
```python
import math
import jax
import jax.numpy as jnp
from jax import lax
from jax.sharding import PartitionSpec as P

D = 1024
HEADS = 16
KV_HEADS = 8
HEAD_DIM = 64
EXPERTS = 32
TOPK = 8
CAP = 48
EPS = 1e-06
RESIDUAL = 0.22
ATT_SCALE = 0.015625
ROPE_BASE = 10000.0
NEG = -1000000000.0


def phases(segment):
    length = segment.shape[0]
    places = jnp.arange(length, dtype=jnp.int32)
    starts = jnp.concatenate([jnp.ones((1,), dtype=bool), segment[1:] != segment[:-1]])
    opening = lax.cummax(jnp.where(starts, places, 0), axis=0)
    offset = (places - opening).astype(jnp.float32)
    halves = HEAD_DIM // 2
    frequency = jnp.exp(
        -math.log(ROPE_BASE) * 2.0 * jnp.arange(halves).astype(jnp.float32) / HEAD_DIM
    )
    angles = offset[:, None] * frequency[None, :]
    angles = jnp.concatenate([angles, angles], axis=1)[:, None, :]
    visible = (places[None, :] <= places[:, None]) & (segment[:, None] == segment[None, :])
    return (jnp.cos(angles), jnp.sin(angles), visible)


def rotate(values, cos_table, sin_table):
    height = values.shape[0]
    per_head = values.reshape(height, -1, HEAD_DIM)
    halves = HEAD_DIM // 2
    turned = jnp.concatenate([-per_head[..., halves:], per_head[..., :halves]], axis=-1)
    return (per_head * cos_table + turned * sin_table).reshape(height, -1)


def slot_index(route_ids):
    flat_routes = route_ids.reshape(-1)
    choose = (flat_routes[:, None] == jnp.arange(EXPERTS, dtype=jnp.int32)[None, :]).astype(
        jnp.int32
    )
    before = jnp.cumsum(choose, axis=0) - choose
    slots = jnp.sum(before * choose, axis=1)
    return flat_routes * CAP + slots


def normalize(values, gain):
    scale = lax.rsqrt(jnp.mean(values * values, axis=-1, keepdims=True) + EPS)
    normed = values * scale
    return (normed, scale, normed * gain)


def normalize_back(grad_out, normed, scale, gain):
    grad_norm = grad_out * gain
    grad_in = scale * (grad_norm - normed * jnp.mean(grad_norm * normed, axis=-1, keepdims=True))
    return (grad_in, jnp.sum(grad_out * normed, axis=0))


def scores_of(query_low, key_low, visible):
    height = query_low.shape[0]
    query_four = query_low.reshape(height, KV_HEADS, HEADS // KV_HEADS, HEAD_DIM)
    key_three = key_low.reshape(height, KV_HEADS, HEAD_DIM)
    scores = (
        jnp.einsum("qkgd,skd->kgqs", query_four, key_three, preferred_element_type=jnp.float32)
        * ATT_SCALE
    )
    return jnp.where(visible[None, None], scores, NEG)


def attend(query_low, key_low, value_low, visible):
    height = query_low.shape[0]
    scores = scores_of(query_low, key_low, visible)
    highest = jnp.max(scores, axis=-1, keepdims=True)
    log_total = highest + jnp.log(jnp.sum(jnp.exp(scores - highest), axis=-1, keepdims=True))
    attention = jnp.exp(scores - log_total).astype(jnp.bfloat16)
    value_three = value_low.reshape(height, KV_HEADS, HEAD_DIM)
    attended = jnp.einsum(
        "kgqs,skd->qkgd", attention, value_three, preferred_element_type=jnp.float32
    )
    return (attended.reshape(height, -1).astype(jnp.bfloat16), log_total)


def attend_back(query_low, key_low, value_low, visible, log_total, grad_mixed):
    height = query_low.shape[0]
    query_four = query_low.reshape(height, KV_HEADS, HEADS // KV_HEADS, HEAD_DIM)
    key_three = key_low.reshape(height, KV_HEADS, HEAD_DIM)
    value_three = value_low.reshape(height, KV_HEADS, HEAD_DIM)
    attention = jnp.exp(scores_of(query_low, key_low, visible) - log_total)
    attention_low = attention.astype(jnp.bfloat16)
    grad_four = grad_mixed.reshape(height, KV_HEADS, HEADS // KV_HEADS, HEAD_DIM)
    value_grad = jnp.einsum(
        "kgqs,qkgd->skd", attention_low, grad_four, preferred_element_type=jnp.float32
    )
    prob_grad = jnp.einsum(
        "qkgd,skd->kgqs", grad_four, value_three, preferred_element_type=jnp.float32
    )
    inner_prod = jnp.sum(attention * prob_grad, axis=-1, keepdims=True)
    score_grad = (attention * (prob_grad - inner_prod)).astype(jnp.bfloat16)
    query_grad = (
        jnp.einsum("kgqs,skd->qkgd", score_grad, key_three, preferred_element_type=jnp.float32)
        * ATT_SCALE
    )
    key_grad = (
        jnp.einsum("kgqs,qkgd->skd", score_grad, query_four, preferred_element_type=jnp.float32)
        * ATT_SCALE
    )
    return (
        query_grad.reshape(height, -1),
        key_grad.reshape(height, -1),
        value_grad.reshape(height, -1),
    )


def fetch_dense(attn_gain, moe_gain, w_query, w_key, w_value, w_output, w_router):
    return (
        lax.all_gather(attn_gain, "fsdp", axis=0, tiled=True),
        lax.all_gather(moe_gain, "fsdp", axis=0, tiled=True),
        lax.all_gather(w_query, "fsdp", axis=0, tiled=True),
        lax.all_gather(w_key, "fsdp", axis=0, tiled=True),
        lax.all_gather(w_value, "fsdp", axis=0, tiled=True),
        lax.all_gather(w_output, "fsdp", axis=0, tiled=True),
        lax.all_gather(w_router, "fsdp", axis=0, tiled=True),
    )


def reduce_dense(grads):
    return (
        lax.psum_scatter(grads[0], "fsdp", scatter_dimension=0, tiled=True),
        lax.psum_scatter(grads[1], "fsdp", scatter_dimension=0, tiled=True),
        lax.psum_scatter(grads[2], "fsdp", scatter_dimension=0, tiled=True),
        lax.psum_scatter(grads[3], "fsdp", scatter_dimension=0, tiled=True),
        lax.psum_scatter(grads[4], "fsdp", scatter_dimension=0, tiled=True),
        lax.psum_scatter(grads[5], "fsdp", scatter_dimension=0, tiled=True),
        lax.psum_scatter(grads[6], "fsdp", scatter_dimension=0, tiled=True),
    )


def combine_sum(current, update):
    return current + update


def on_device(
    tokens,
    segments,
    routes,
    cotangent,
    attn_gain,
    moe_gain,
    w_query,
    w_key,
    w_value,
    w_output,
    w_router,
    w_gate,
    w_up,
    w_down,
):
    micro = tokens.shape[0]
    length = tokens.shape[2]
    groups = lax.axis_size("fsdp")
    local_experts = w_gate.shape[0]
    shards = (attn_gain, moe_gain, w_query, w_key, w_value, w_output, w_router)
    totals = tuple((jnp.zeros(member.shape, jnp.float32) for member in shards))
    grad_gate = jnp.zeros(w_gate.shape, jnp.float32)
    grad_up = jnp.zeros(w_up.shape, jnp.float32)
    grad_down = jnp.zeros(w_down.shape, jnp.float32)
    outputs = []
    grads_in = []
    expert_ids = jnp.arange(EXPERTS, dtype=jnp.int32)
    for number in range(micro):
        dense_set = fetch_dense(attn_gain, moe_gain, w_query, w_key, w_value, w_output, w_router)
        gain_one = dense_set[0].astype(jnp.float32)
        gain_two = dense_set[1].astype(jnp.float32)
        inputs = tokens[number, 0].astype(jnp.float32)
        segment = segments[number, 0]
        route_ids = routes[number, 0]
        cos_table, sin_table, visible = phases(segment)
        normed_one, scale_one, hidden_one = normalize(inputs, gain_one)
        hidden_low = hidden_one.astype(jnp.bfloat16)
        query_raw = jnp.dot(hidden_low, dense_set[2], preferred_element_type=jnp.float32)
        key_raw = jnp.dot(hidden_low, dense_set[3], preferred_element_type=jnp.float32)
        value_low = jnp.dot(hidden_low, dense_set[4], preferred_element_type=jnp.float32).astype(
            jnp.bfloat16
        )
        query_low = rotate(query_raw, cos_table, sin_table).astype(jnp.bfloat16)
        key_low = rotate(key_raw, cos_table, sin_table).astype(jnp.bfloat16)
        mixed_low, log_total = attend(query_low, key_low, value_low, visible)
        branch = jnp.dot(mixed_low, dense_set[5], preferred_element_type=jnp.float32)
        middle = inputs + RESIDUAL * branch
        normed_two, scale_two, hidden_two = normalize(middle, gain_two)
        routed_low = hidden_two.astype(jnp.bfloat16)
        logits = jnp.dot(routed_low, dense_set[6], preferred_element_type=jnp.float32)
        choose = (route_ids[:, :, None] == expert_ids[None, None, :]).astype(jnp.float32)
        chosen = jnp.einsum("tke,te->tk", choose, logits)
        gate_weights = jax.nn.softmax(chosen, axis=-1)
        places = slot_index(route_ids)
        copies = jnp.repeat(routed_low, TOPK, axis=0)
        outgoing = (
            jnp.zeros((EXPERTS * CAP, D), jnp.bfloat16)
            .at[places]
            .set(copies)
            .reshape(EXPERTS, CAP, D)
        )
        arrived = lax.all_to_all(outgoing, "fsdp", split_axis=0, concat_axis=0, tiled=True).reshape(
            groups, local_experts, CAP, D
        )
        gate_act = jnp.einsum("secd,edf->secf", arrived, w_gate, preferred_element_type=jnp.float32)
        up_act = jnp.einsum("secd,edf->secf", arrived, w_up, preferred_element_type=jnp.float32)
        sigmoid_act = jax.nn.sigmoid(gate_act)
        swish_act = gate_act * sigmoid_act
        inner_low = (swish_act * up_act).astype(jnp.bfloat16)
        expert_out = jnp.einsum(
            "secf,efd->secd", inner_low, w_down, preferred_element_type=jnp.float32
        ).astype(jnp.bfloat16)
        returned = lax.all_to_all(
            expert_out.reshape(groups * local_experts, CAP, D),
            "fsdp",
            split_axis=0,
            concat_axis=0,
            tiled=True,
        ).reshape(EXPERTS * CAP, D)
        picked = returned[places].reshape(length, TOPK, D)
        mixture = jnp.sum(gate_weights[:, :, None] * picked, axis=1)
        result = middle + RESIDUAL * mixture
        outputs.append(result.astype(jnp.bfloat16))
        dense_set = fetch_dense(attn_gain, moe_gain, w_query, w_key, w_value, w_output, w_router)
        upstream = cotangent[number, 0].astype(jnp.float32)
        grad_mix = RESIDUAL * upstream
        gate_grad = jnp.sum(picked * grad_mix[:, None, :], axis=-1)
        slot_grad = (
            (gate_weights[:, :, None] * grad_mix[:, None, :])
            .astype(jnp.bfloat16)
            .reshape(length * TOPK, D)
        )
        sending = (
            jnp.zeros((EXPERTS * CAP, D), jnp.bfloat16)
            .at[places]
            .set(slot_grad)
            .reshape(EXPERTS, CAP, D)
        )
        arrived_grad = lax.all_to_all(
            sending, "fsdp", split_axis=0, concat_axis=0, tiled=True
        ).reshape(groups, local_experts, CAP, D)
        inner_grad = jnp.einsum(
            "secd,efd->secf", arrived_grad, w_down, preferred_element_type=jnp.float32
        )
        grad_down = grad_down + jnp.einsum(
            "secf,secd->efd", inner_low, arrived_grad, preferred_element_type=jnp.float32
        )
        gate_pre = (
            inner_grad * up_act * sigmoid_act * (1.0 + gate_act * (1.0 - sigmoid_act))
        ).astype(jnp.bfloat16)
        up_pre = (inner_grad * swish_act).astype(jnp.bfloat16)
        grad_gate = grad_gate + jnp.einsum(
            "secd,secf->edf", arrived, gate_pre, preferred_element_type=jnp.float32
        )
        grad_up = grad_up + jnp.einsum(
            "secd,secf->edf", arrived, up_pre, preferred_element_type=jnp.float32
        )
        feature_grad = jnp.einsum(
            "secf,edf->secd", gate_pre, w_gate, preferred_element_type=jnp.float32
        )
        feature_grad = feature_grad + jnp.einsum(
            "secf,edf->secd", up_pre, w_up, preferred_element_type=jnp.float32
        )
        back_rows = lax.all_to_all(
            feature_grad.astype(jnp.bfloat16).reshape(groups * local_experts, CAP, D),
            "fsdp",
            split_axis=0,
            concat_axis=0,
            tiled=True,
        ).reshape(EXPERTS * CAP, D)
        routed_grad = jnp.sum(
            back_rows[places].reshape(length, TOPK, D).astype(jnp.float32), axis=1
        )
        choice_grad = gate_weights * (
            gate_grad - jnp.sum(gate_weights * gate_grad, axis=-1, keepdims=True)
        )
        logit_grad = jnp.einsum("tke,tk->te", choose, choice_grad).astype(jnp.bfloat16)
        router_grad = jnp.einsum(
            "td,te->de", routed_low, logit_grad, preferred_element_type=jnp.float32
        )
        routed_grad = routed_grad + jnp.einsum(
            "te,de->td", logit_grad, dense_set[6], preferred_element_type=jnp.float32
        )
        middle_grad, gain_two_grad = normalize_back(routed_grad, normed_two, scale_two, gain_two)
        middle_grad = middle_grad + upstream
        branch_low = (RESIDUAL * middle_grad).astype(jnp.bfloat16)
        output_grad = jnp.einsum(
            "tf,td->fd", mixed_low, branch_low, preferred_element_type=jnp.float32
        )
        mixed_grad = jnp.einsum(
            "td,fd->tf", branch_low, dense_set[5], preferred_element_type=jnp.float32
        ).astype(jnp.bfloat16)
        query_grad, key_grad, value_grad = attend_back(
            query_low, key_low, value_low, visible, log_total, mixed_grad
        )
        query_low_grad = rotate(query_grad, cos_table, -sin_table).astype(jnp.bfloat16)
        key_low_grad = rotate(key_grad, cos_table, -sin_table).astype(jnp.bfloat16)
        value_low_grad = value_grad.astype(jnp.bfloat16)
        wq_grad = jnp.einsum(
            "td,tf->df", hidden_low, query_low_grad, preferred_element_type=jnp.float32
        )
        wk_grad = jnp.einsum(
            "td,tf->df", hidden_low, key_low_grad, preferred_element_type=jnp.float32
        )
        wv_grad = jnp.einsum(
            "td,tf->df", hidden_low, value_low_grad, preferred_element_type=jnp.float32
        )
        hidden_grad = jnp.einsum(
            "tf,df->td", query_low_grad, dense_set[2], preferred_element_type=jnp.float32
        )
        hidden_grad = hidden_grad + jnp.einsum(
            "tf,df->td", key_low_grad, dense_set[3], preferred_element_type=jnp.float32
        )
        hidden_grad = hidden_grad + jnp.einsum(
            "tf,df->td", value_low_grad, dense_set[4], preferred_element_type=jnp.float32
        )
        normed_grad, gain_one_grad = normalize_back(hidden_grad, normed_one, scale_one, gain_one)
        grads_in.append(middle_grad + normed_grad)
        dense_grads = (
            gain_one_grad,
            gain_two_grad,
            wq_grad,
            wk_grad,
            wv_grad,
            output_grad,
            router_grad,
        )
        reduced = reduce_dense(dense_grads)
        totals = tuple((combine_sum(current, update) for current, update in zip(totals, reduced)))
    summed = lax.psum(
        (
            totals[0],
            totals[1],
            totals[2],
            totals[3],
            totals[4],
            totals[5],
            totals[6],
            grad_gate,
            grad_up,
            grad_down,
        ),
        "rep",
    )
    return (
        jnp.stack(outputs)[:, None],
        jnp.stack(grads_in)[:, None],
        summed[0],
        summed[1],
        summed[2],
        summed[3],
        summed[4],
        summed[5],
        summed[6],
        summed[7],
        summed[8],
        summed[9],
    )


def solution(mesh):
    placed = (
        P(None, ("rep", "fsdp"), None, None),
        P(None, ("rep", "fsdp"), None),
        P(None, ("rep", "fsdp"), None, None),
        P(None, ("rep", "fsdp"), None, None),
        P("fsdp"),
        P("fsdp"),
        P("fsdp", None),
        P("fsdp", None),
        P("fsdp", None),
        P("fsdp", None),
        P("fsdp", None),
        P("fsdp", None, None),
        P("fsdp", None, None),
        P("fsdp", None, None),
    )
    return jax.shard_map(
        on_device,
        mesh=mesh,
        in_specs=placed,
        out_specs=(
            P(None, ("rep", "fsdp"), None, None),
            P(None, ("rep", "fsdp"), None, None),
            P("fsdp"),
            P("fsdp"),
            P("fsdp", None),
            P("fsdp", None),
            P("fsdp", None),
            P("fsdp", None),
            P("fsdp", None),
            P("fsdp", None, None),
            P("fsdp", None, None),
            P("fsdp", None, None),
        ),
        check_vma=False,
    )
```

profile of v0, /device:TPU:1, one launch (start us, length us, event | category | flops | bytes accessed | tf_op | source)
XLA Modules:
  0.0 1932.4 jit_solution(3319828074950691068)
XLA Ops:
  16.1 84.6 %all-reduce.7 = (bf16[1024]{0:T(1024)(128)(2,1)S(1)}, bf16[1024]{0:T(1024)(128)(2,1)S(1)}) all-reduce(bf16[1024]{0:T(1024)(128)(2,1)S(1)} %dynamic-update-slice, bf16[1024]{0:T(1024)(128)(2,1)S(1)} %dynamic-update-slice.1), channel_id=1, replica_groups=mesh['rep'=4,'fsdp'=32] {'fsdp'}, use_global_device_ids=true, to_apply=%add | all-reduce | flops 2048 | bytes 8192
  117.0 28.5 %all-gather.7.cloned.1.call-done = bf16[1024,512]{1,0:T(8,128)(2,1)} async-done(((bf16[32,512]{1,0:T(8,128)(2,1)}), bf16[1024,512]{1,0:T(8,128)(2,1)}) %all-gather.7.cloned.1.call-update) | async-done | bytes 1048592 | tf_op jit(solution)/shard_map/all_gather | solution.py:127
  147.6 69.3 %all-gather.9.cloned.1.call-done = bf16[1024,1024]{1,0:T(8,128)(2,1)} async-done(((bf16[32,1024]{1,0:T(8,128)(2,1)}), bf16[1024,1024]{1,0:T(8,128)(2,1)}) %all-gather.9.cloned.1.call-update) | async-done | bytes 2097168 | tf_op jit(solution)/shard_map/all_gather | solution.py:126
  225.7 61.9 %all-gather.11.cloned.1.call-done = bf16[1024,1024]{1,0:T(8,128)(2,1)} async-done(((bf16[32,1024]{1,0:T(8,128)(2,1)}), bf16[1024,1024]{1,0:T(8,128)(2,1)}) %all-gather.11.cloned.1.call-update) | async-done | bytes 2097168 | tf_op jit(solution)/shard_map/all_gather | solution.py:129
  303.7 107.3 %all_gather.20 = bf16[1024,32]{1,0:T(8,128)(2,1)S(1)} all-gather(bf16[32,32]{1,0:T(8,128)(2,1)S(1)} %copy-done.108), channel_id=1, replica_groups=mesh['rep'=4,'fsdp'=32] {'fsdp'}, dimensions={0}, use_global_device_ids=true | all-gather | bytes 67584 | tf_op jit(solution)/shard_map/all_gather | solution.py:130
  437.6 23.1 %all-to-all-done.4 = bf16[32,48,1024]{2,1,0:T(8,128)(2,1)} async-done(((bf16[32,48,1024]{2,1,0:T(8,128)(2,1)}), bf16[32,48,1024]{2,1,0:T(8,128)(2,1)}, u32[]{:S(2)}, u32[]{:S(2)}) %all-to-all-start.4) | async-done | bytes 3145760 | tf_op jit(solution)/shard_map/all_to_all | solution.py:249
  476.0 13.0 all-to-all-start.1
  510.8 13.0 all-to-all-done.1
  523.8 22.2 %all-to-all-start.5 = ((bf16[32,48,1024]{2,1,0:T(8,128)(2,1)}), bf16[32,48,1024]{2,1,0:T(8,128)(2,1)}, u32[]{:S(2)}, u32[]{:S(2)}) async-start(bf16[32,48,1024]{2,1,0:T(8,128)(2,1)} %add_convert_fusion.1), calls=%async_computation.5 | async-start | bytes 6291456 | tf_op jit(solution)/shard_map/all_to_all | solution.py:274
  563.9 18.4 all-to-all-done.5
  601.8 13.1 all-to-all-start.2
  624.4 30.1 %all-to-all-done.2 = bf16[32,48,1024]{2,1,0:T(8,128)(2,1)} async-done(((bf16[32,48,1024]{2,1,0:T(8,128)(2,1)}), bf16[32,48,1024]{2,1,0:T(8,128)(2,1)}, u32[]{:S(2)}, u32[]{:S(2)}) %all-to-all-start.2) | async-done | bytes 3145760 | tf_op jit(solution)/shard_map/all_to_all | solution.py:212
  670.5 34.6 %all-to-all-done.6 = bf16[32,48,1024]{2,1,0:T(8,128)(2,1)} async-done(((bf16[32,48,1024]{2,1,0:T(8,128)(2,1)}), bf16[32,48,1024]{2,1,0:T(8,128)(2,1)}, u32[]{:S(2)}, u32[]{:S(2)}) %all-to-all-start.6) | async-done | bytes 3145760 | tf_op jit(solution)/shard_map/all_to_all | solution.py:249
  737.3 33.3 %all-to-all-done.3 = bf16[32,48,1024]{2,1,0:T(8,128)(2,1)} async-done(((bf16[32,48,1024]{2,1,0:T(8,128)(2,1)}), bf16[32,48,1024]{2,1,0:T(8,128)(2,1)}, u32[]{:S(2)}, u32[]{:S(2)}) %all-to-all-start.3) | async-done | bytes 3145760 | tf_op jit(solution)/shard_map/all_to_all | solution.py:223
  770.7 10.6 all-to-all-start.7
  795.2 27.0 %all-to-all-done.7 = bf16[32,48,1024]{2,1,0:T(8,128)(2,1)S(1)} async-done(((bf16[32,48,1024]{2,1,0:T(8,128)(2,1)}), bf16[32,48,1024]{2,1,0:T(8,128)(2,1)S(1)}, u32[]{:S(2)}, u32[]{:S(2)}) %all-to-all-start.7) | async-done | bytes 3145760 | tf_op jit(solution)/shard_map/all_to_all | solution.py:274
  895.4 114.7 %reduce-scatter.10.cloned.1.call-done = f32[32,512]{1,0:T(8,128)} async-done(((f32[1024,512]{1,0:T(8,128)}), f32[32,512]{1,0:T(8,128)}) %reduce-scatter.10.cloned.1.call-update) | async-done | bytes 65552 | tf_op jit(solution)/shard_map/reduce_scatter | solution.py:140
  1010.2 184.8 %reduce-scatter.8.cloned.1.call-done = f32[32,512]{1,0:T(8,128)} async-done(((f32[1024,512]{1,0:T(8,128)}), f32[32,512]{1,0:T(8,128)}) %reduce-scatter.8.cloned.1.call-update) | async-done | bytes 65552 | tf_op jit(solution)/shard_map/reduce_scatter | solution.py:139
  1195.0 191.4 %reduce-scatter.12.cloned.1.call-done = f32[32,1024]{1,0:T(8,128)} async-done(((f32[1024,1024]{1,0:T(8,128)}), f32[32,1024]{1,0:T(8,128)}) %reduce-scatter.12.cloned.1.call-update) | async-done | bytes 131088 | tf_op jit(solution)/shard_map/reduce_scatter | solution.py:141
  1386.4 189.5 %reduce-scatter.6.cloned.1.call-done = f32[32,1024]{1,0:T(8,128)} async-done(((f32[1024,1024]{1,0:T(8,128)}), f32[32,1024]{1,0:T(8,128)}) %reduce-scatter.6.cloned.1.call-update) | async-done | bytes 131088 | tf_op jit(solution)/shard_map/reduce_scatter | solution.py:138
  1584.7 77.8 %all-reduce.4 = (f32[1024]{0:T(1024)S(1)}, f32[1024]{0:T(1024)S(1)}) all-reduce(f32[1024]{0:T(1024)S(1)} %add.332, f32[1024]{0:T(1024)S(1)} %copy-done.96), channel_id=9, replica_groups=mesh['rep'=4,'fsdp'=32] {'fsdp'}, use_global_device_ids=true, to_apply=%region_39.40.clone | all-reduce | flops 2048 | bytes 16384
  1665.9 89.4 %reduce-scatter.14.cloned.1.call-done = f32[32,32]{1,0:T(8,128)} async-done(((f32[1024,32]{1,0:T(8,128)}), f32[32,32]{1,0:T(8,128)}) %reduce-scatter.14.cloned.1.call-update) | async-done | bytes 4112 | tf_op jit(solution)/shard_map/reduce_scatter | solution.py:142
  1755.2 36.6 %all-reduce.5 = (f32[32]{0:T(128)}, f32[32]{0:T(128)}, f32[32,32]{1,0:T(8,128)}) all-reduce(f32[32]{0:T(128)S(1)} %dynamic-slice.3, f32[32]{0:T(128)S(1)} %dynamic-slice.5, f32[32,32]{1,0:T(8,128)} %reduce-scatter.14.cloned.1.call-done), channel_id=1, replica_groups=mesh['rep'=4,'fsdp'=32] {'rep'}, use_global_device_ids=true, to_apply=%region_42.43 | all-reduce | flops 1088 | bytes 8704 | tf_op jit(solution)/shard_map/psum | solution.py:340
  1791.8 120.3 %all-reduce.10.cloned.1.call-done = (f32[32,1024]{1,0:T(8,128)}, f32[32,512]{1,0:T(8,128)}, f32[32,512]{1,0:T(8,128)}, f32[32,1024]{1,0:T(8,128)}, f32[1,1024,51...) async-done(((f32[32,1024]{1,0:T(8,128)}, f32[32,512]{1,0:T(8,128)}, f32[32,512]{1,0:T(8,128)}, f32[32,1024]{1,0:T(8,128)}, f32[1,1024,512]{2,1,0:T(8,128)}, ...) | async-done | bytes 6684688 | tf_op jit(solution)/shard_map/psum | solution.py:340
  (477 shorter events, 319.8 us)
Async XLA Ops:
  7.2 457.7 %copy-start = (bf16[1,1024,512]{2,1,0:T(8,128)(2,1)S(1)}, bf16[1,1024,512]{2,1,0:T(8,128)(2,1)}, u32[]{:S(2)}) copy-start(bf16[1,1024,512]{2,1,0:T(8,128)(2,1)} %param.25) | copy-start | bytes 3145732
  7.2 106.8 %copy-start.103 = (s32[2,1,128]{2,1,0:T(1,128)S(1)}, s32[2,1,128]{2,1,0:T(1,128)}, u32[]{:S(2)}) copy-start(s32[2,1,128]{2,1,0:T(1,128)} %param.15) | copy-start | bytes 3076
  7.2 108.0 %copy-start.2 = (bf16[2,1,128,1024]{3,2,1,0:T(8,128)(2,1)S(1)}, bf16[2,1,128,1024]{3,2,1,0:T(8,128)(2,1)}, u32[]{:S(2)}) copy-start(bf16[2,1,128,1024]{3,2,1,0:T(8,128)(2,1)} %param.14) | copy-start | bytes 1572868
  7.2 108.0 %all-gather.5.cloned.1.call-start = ((), (), s32[]{:S(2)}) async-start(), calls=%async_computation.13 | async-start | bytes 1081344 | tf_op jit(solution)/shard_map/all_gather | solution.py:128
  8.0 137.5 %all-gather.7.cloned.1.call-start = ((), (), s32[]{:S(2)}) async-start(), calls=%async_computation.14 | async-start | bytes 1081344 | tf_op jit(solution)/shard_map/all_gather | solution.py:127
  8.7 208.1 %all-gather.9.cloned.1.call-start = ((), (), s32[]{:S(2)}) async-start(), calls=%async_computation.15 | async-start | bytes 2162688 | tf_op jit(solution)/shard_map/all_gather | solution.py:126
  9.4 278.1 %all-gather.11.cloned.1.call-start = ((), (), s32[]{:S(2)}) async-start(), calls=%async_computation.16 | async-start | bytes 2162688 | tf_op jit(solution)/shard_map/all_gather | solution.py:129
  103.2 120.0 %copy-start.68 = (f32[128,64]{0,1:T(8,128)}, f32[128,64]{0,1:T(8,128)S(1)}, u32[]{:S(2)}) copy-start(f32[128,64]{0,1:T(8,128)S(1)} %get-tuple-element.115) | copy-start | bytes 98308
  114.5 176.1 %copy-start.94 = (s32[1024,1]{0,1:T(1,128)}, s32[1024,1]{0,1:T(1,128)S(1)}, u32[]{:S(2)}) copy-start(s32[1024,1]{0,1:T(1,128)S(1)} %compare_select_fusion.1) | copy-start | bytes 12292
  116.9 107.6 %copy-start.50 = (bf16[128,512]{0,1:T(8,128)(2,1)}, bf16[128,512]{0,1:T(8,128)(2,1)S(1)}, u32[]{:S(2)}) copy-start(bf16[128,512]{0,1:T(8,128)(2,1)S(1)} %copy.80) | copy-start | bytes 393220
  298.0 128.3 %all-to-all-start = ((bf16[32,48,1024]{2,1,0:T(8,128)(2,1)}), bf16[32,48,1024]{2,1,0:T(8,128)(2,1)}, u32[]{:S(2)}, u32[]{:S(2)}) async-start(bf16[32,48,1024]{2,1,0:T(8,128)(2,1)} %bitcast.622), calls=%async_computation | async-start | bytes 6291456 | tf_op jit(solution)/shard_map/all_to_all | solution.py:212
  426.3 34.4 %all-to-all-start.4 = ((bf16[32,48,1024]{2,1,0:T(8,128)(2,1)}), bf16[32,48,1024]{2,1,0:T(8,128)(2,1)}, u32[]{:S(2)}, u32[]{:S(2)}) async-start(bf16[32,48,1024]{2,1,0:T(8,128)(2,1)} %bitcast.624), calls=%async_computation.4 | async-start | bytes 6291456 | tf_op jit(solution)/shard_map/all_to_all | solution.py:249
  476.0 47.8 %all-to-all-start.1 = ((bf16[32,48,1024]{2,1,0:T(8,128)(2,1)}), bf16[32,48,1024]{2,1,0:T(8,128)(2,1)}, u32[]{:S(2)}, u32[]{:S(2)}) async-start(bf16[32,48,1024]{2,1,0:T(8,128)(2,1)} %convolution_convert_fusion.1), calls=%async_computation.1 | async-start | bytes 6291456 | tf_op jit(solution)/shard_map/all_to_all | solution.py:223
  523.8 58.5 %all-to-all-start.5 = ((bf16[32,48,1024]{2,1,0:T(8,128)(2,1)}), bf16[32,48,1024]{2,1,0:T(8,128)(2,1)}, u32[]{:S(2)}, u32[]{:S(2)}) async-start(bf16[32,48,1024]{2,1,0:T(8,128)(2,1)} %add_convert_fusion.1), calls=%async_computation.5 | async-start | bytes 6291456 | tf_op jit(solution)/shard_map/all_to_all | solution.py:274
  601.8 52.7 %all-to-all-start.2 = ((bf16[32,48,1024]{2,1,0:T(8,128)(2,1)}), bf16[32,48,1024]{2,1,0:T(8,128)(2,1)}, u32[]{:S(2)}, u32[]{:S(2)}) async-start(bf16[32,48,1024]{2,1,0:T(8,128)(2,1)} %bitcast.623), calls=%async_computation.2 | async-start | bytes 6291456 | tf_op jit(solution)/shard_map/all_to_all | solution.py:212
  654.5 50.6 %all-to-all-start.6 = ((bf16[32,48,1024]{2,1,0:T(8,128)(2,1)}), bf16[32,48,1024]{2,1,0:T(8,128)(2,1)}, u32[]{:S(2)}, u32[]{:S(2)}) async-start(bf16[32,48,1024]{2,1,0:T(8,128)(2,1)} %bitcast.625), calls=%async_computation.6 | async-start | bytes 6291456 | tf_op jit(solution)/shard_map/all_to_all | solution.py:249
  720.0 50.7 %all-to-all-start.3 = ((bf16[32,48,1024]{2,1,0:T(8,128)(2,1)}), bf16[32,48,1024]{2,1,0:T(8,128)(2,1)}, u32[]{:S(2)}, u32[]{:S(2)}) async-start(bf16[32,48,1024]{2,1,0:T(8,128)(2,1)} %convolution_convert_fusion), calls=%async_computation.3 | async-start | bytes 6291456 | tf_op jit(solution)/shard_map/all_to_all | solution.py:223
  770.7 51.5 %all-to-all-start.7 = ((bf16[32,48,1024]{2,1,0:T(8,128)(2,1)}), bf16[32,48,1024]{2,1,0:T(8,128)(2,1)S(1)}, u32[]{:S(2)}, u32[]{:S(2)}) async-start(bf16[32,48,1024]{2,1,0:T(8,128)(2,1)} %add_convert_fusion), calls=%async_computation.7 | async-start | bytes 6291456 | tf_op jit(solution)/shard_map/all_to_all | solution.py:274
  781.3 228.8 %reduce-scatter.10.cloned.1.call-start = ((), (), s32[]{:S(2)}) async-start(), calls=%async_computation.19 | async-start | bytes 2162688 | tf_op jit(solution)/shard_map/reduce_scatter | solution.py:140
  846.1 348.9 %reduce-scatter.8.cloned.1.call-start = ((), (), s32[]{:S(2)}) async-start(), calls=%async_computation.18 | async-start | bytes 2162688 | tf_op jit(solution)/shard_map/reduce_scatter | solution.py:139
  852.7 533.7 %reduce-scatter.12.cloned.1.call-start = ((), (), s32[]{:S(2)}) async-start(), calls=%async_computation.20 | async-start | bytes 4325376 | tf_op jit(solution)/shard_map/reduce_scatter | solution.py:141
  856.5 719.4 %reduce-scatter.6.cloned.1.call-start = ((), (), s32[]{:S(2)}) async-start(), calls=%async_computation.17 | async-start | bytes 4325376 | tf_op jit(solution)/shard_map/reduce_scatter | solution.py:138
  863.9 891.3 %reduce-scatter.14.cloned.1.call-start = ((), (), s32[]{:S(2)}) async-start(), calls=%async_computation.21 | async-start | bytes 540672 | tf_op jit(solution)/shard_map/reduce_scatter | solution.py:142
  888.9 1023.2 %all-reduce.10.cloned.1.call-start = ((), (), s32[]{:S(2)}) async-start(), calls=%async_computation.22 | async-start | bytes 13369344 | tf_op jit(solution)/shard_map/psum | solution.py:340
  (118 other events, 1443.1 us)
Sparse Core Ops, SparseCore 0:
  11.0 67.9 all-gather.4
  82.0 63.4 all-gather.6
  148.6 68.2 all-gather.8
  219.8 67.6 all-gather.10
  846.2 163.9 reduce-scatter.9
  1013.1 181.8 reduce-scatter.7
  1197.3 188.9 reduce-scatter.11
  1388.8 187.0 reduce-scatter.5
  1578.2 176.9 reduce-scatter.13
  1759.0 153.0 all-reduce.9
where the time goes:
time: 1940 us; the launch traced here: 1930 us
  waiting for transfers between devices  1230 us (63%)
  blocking collectives  306 us (16%)
  matrix products  132 us (7%)
  starting transfers between devices  90.4 us (5%)
  local copies, waits for them, and re-layouts  81.1 us (4%)
  other arithmetic  72.8 us (4%)
    reduce_scatter x1, waiting for transfers between devices, reduce_dense(): lax.psum_scatter(grads[5], 'fsdp', scatter_dimension=0, tiled=True)  191 us
    reduce_scatter x1, waiting for transfers between devices, reduce_dense(): lax.psum_scatter(grads[2], 'fsdp', scatter_dimension=0, tiled=True)  189 us
    reduce_scatter x1, waiting for transfers between devices, reduce_dense(): lax.psum_scatter(grads[3], 'fsdp', scatter_dimension=0, tiled=True)  185 us
    unnamed x2, blocking collectives  162 us
    psum x1, waiting for transfers between devices, on_device(): lax.psum((totals[0], totals[1], totals[2], totals[3], totals[4], totals[5...  120 us
    reduce_scatter x1, waiting for transfers between devices, reduce_dense(): lax.psum_scatter(grads[4], 'fsdp', scatter_dimension=0, tiled=True)  115 us
    all_gather x1, blocking collectives, fetch_dense(): lax.all_gather(w_router, 'fsdp', axis=0, tiled=True)  107 us
    reduce_scatter x1, waiting for transfers between devices, reduce_dense(): lax.psum_scatter(grads[6], 'fsdp', scatter_dimension=0, tiled=True)  89.4 us
  transfers between devices with their start and end apart: 18, of which 16 were waited for; matrix products, arithmetic and copies ran while one was open for 9% of the time, Pallas kernels for 0%

commit v1 on v0

--- a/solution.py
+++ b/solution.py
@@ -18,6 +18,13 @@
 NEG = -1000000000.0
 
 
+def patch_wait(vector, at_axis):
+    return jnp.concatenate(
+        jax.lax.all_to_all(jnp.stack(jax.lax.axis_size("fsdp") * [vector], axis=0), "fsdp", 0, 0),
+        at_axis,
+    )
+
+
 def phases(segment):
     length = segment.shape[0]
     places = jnp.arange(length, dtype=jnp.int32)
@@ -127,7 +134,7 @@
         lax.all_gather(w_key, "fsdp", axis=0, tiled=True),
         lax.all_gather(w_value, "fsdp", axis=0, tiled=True),
         lax.all_gather(w_output, "fsdp", axis=0, tiled=True),
-        lax.all_gather(w_router, "fsdp", axis=0, tiled=True),
+        patch_wait(w_router, 0),
     )
 
 

time: 1940 us -> 1880 us (0.969)
  blocking collectives: 306 us -> 197 us
  waiting for transfers between devices: 1230 us -> 1270 us
    all_gather x1 -> x0, blocking collectives: 107 us -> none  [fetch_dense(): lax.all_gather(w_router, 'fsdp', axis=0, tiled=True)]
    all_to_all x2, waiting for transfers between devices: 30.1 us -> 54.2 us  [on_device(): lax.all_to_all(outgoing, 'fsdp', split_axis=0, concat_axis=0, tiled=True)]
  transfers between devices with their start and end apart: 18 -> 19, of which waited for: 16 -> 17; matrix products, arithmetic and copies ran while one was open for 9% -> 10% of each run, Pallas kernels for 0% -> 0%
where the time goes in v1:
time: 1880 us; the launch traced here: 1870 us
  waiting for transfers between devices  1270 us (68%)
  blocking collectives  197 us (10%)
  matrix products  132 us (7%)
  starting transfers between devices  99.6 us (5%)
  local copies, waits for them, and re-layouts  82.8 us (4%)
  other arithmetic  71.8 us (4%)
    reduce_scatter x1, waiting for transfers between devices, reduce_dense(): lax.psum_scatter(grads[5], 'fsdp', scatter_dimension=0, tiled=True)  191 us
    reduce_scatter x1, waiting for transfers between devices, reduce_dense(): lax.psum_scatter(grads[2], 'fsdp', scatter_dimension=0, tiled=True)  190 us
    reduce_scatter x1, waiting for transfers between devices, reduce_dense(): lax.psum_scatter(grads[3], 'fsdp', scatter_dimension=0, tiled=True)  185 us
    unnamed x2, blocking collectives  160 us
    psum x1, waiting for transfers between devices, on_device(): lax.psum((totals[0], totals[1], totals[2], totals[3], totals[4], totals[5...  120 us
    reduce_scatter x1, waiting for transfers between devices, reduce_dense(): lax.psum_scatter(grads[4], 'fsdp', scatter_dimension=0, tiled=True)  116 us
    reduce_scatter x1, waiting for transfers between devices, reduce_dense(): lax.psum_scatter(grads[6], 'fsdp', scatter_dimension=0, tiled=True)  89.2 us
    all_gather x1, waiting for transfers between devices, fetch_dense(): lax.all_gather(w_query, 'fsdp', axis=0, tiled=True)  69.3 us
  transfers between devices with their start and end apart: 19, of which 17 were waited for; matrix products, arithmetic and copies ran while one was open for 10% of the time, Pallas kernels for 0%

profile of v1, /device:TPU:1, one launch (start us, length us, event | category | flops | bytes accessed | tf_op | source)
XLA Modules:
  0.0 1867.2 jit_solution(7884235925207431253)
XLA Ops:
  11.0 11.3 all-to-all-start
  29.1 82.1 %all-reduce.7 = (bf16[1024]{0:T(1024)(128)(2,1)S(1)}, bf16[1024]{0:T(1024)(128)(2,1)S(1)}) all-reduce(bf16[1024]{0:T(1024)(128)(2,1)S(1)} %dynamic-update-slice, bf16[1024]{0:T(1024)(128)(2,1)S(1)} %dynamic-update-slice.1), channel_id=1, replica_groups=mesh['rep'=4,'fsdp'=32] {'fsdp'}, use_global_device_ids=true, to_apply=%add | all-reduce | flops 2048 | bytes 8192
  126.4 19.1 %all-gather.7.cloned.1.call-done = bf16[1024,512]{1,0:T(8,128)(2,1)} async-done(((bf16[32,512]{1,0:T(8,128)(2,1)}), bf16[1024,512]{1,0:T(8,128)(2,1)}) %all-gather.7.cloned.1.call-update) | async-done | bytes 1048592 | tf_op jit(solution)/shard_map/all_gather | solution.py:134
  147.6 69.3 %all-gather.9.cloned.1.call-done = bf16[1024,1024]{1,0:T(8,128)(2,1)} async-done(((bf16[32,1024]{1,0:T(8,128)(2,1)}), bf16[1024,1024]{1,0:T(8,128)(2,1)}) %all-gather.9.cloned.1.call-update) | async-done | bytes 2097168 | tf_op jit(solution)/shard_map/all_gather | solution.py:133
  225.7 61.9 %all-gather.11.cloned.1.call-done = bf16[1024,1024]{1,0:T(8,128)(2,1)} async-done(((bf16[32,1024]{1,0:T(8,128)(2,1)}), bf16[1024,1024]{1,0:T(8,128)(2,1)}) %all-gather.11.cloned.1.call-update) | async-done | bytes 2097168 | tf_op jit(solution)/shard_map/all_gather | solution.py:136
  319.2 23.5 %all-to-all-done.1 = bf16[32,48,1024]{2,1,0:T(8,128)(2,1)} async-done(((bf16[32,48,1024]{2,1,0:T(8,128)(2,1)}), bf16[32,48,1024]{2,1,0:T(8,128)(2,1)}, u32[]{:S(2)}, u32[]{:S(2)}) %all-to-all-start.1) | async-done | bytes 3145760 | tf_op jit(solution)/shard_map/all_to_all | solution.py:219
  359.5 33.3 %all-to-all-done.5 = bf16[32,48,1024]{2,1,0:T(8,128)(2,1)} async-done(((bf16[32,48,1024]{2,1,0:T(8,128)(2,1)}), bf16[32,48,1024]{2,1,0:T(8,128)(2,1)}, u32[]{:S(2)}, u32[]{:S(2)}) %all-to-all-start.5) | async-done | bytes 3145760 | tf_op jit(solution)/shard_map/all_to_all | solution.py:256
  440.5 17.5 all-to-all-done.2
  458.0 19.6 %all-to-all-start.6 = ((bf16[32,48,1024]{2,1,0:T(8,128)(2,1)}), bf16[32,48,1024]{2,1,0:T(8,128)(2,1)}, u32[]{:S(2)}, u32[]{:S(2)}) async-start(bf16[32,48,1024]{2,1,0:T(8,128)(2,1)} %add_convert_fusion.1), calls=%async_computation.6 | async-start | bytes 6291456 | tf_op jit(solution)/shard_map/all_to_all | solution.py:281
  495.4 22.2 %all-to-all-done.6 = bf16[32,48,1024]{2,1,0:T(8,128)(2,1)} async-done(((bf16[32,48,1024]{2,1,0:T(8,128)(2,1)}), bf16[32,48,1024]{2,1,0:T(8,128)(2,1)}, u32[]{:S(2)}, u32[]{:S(2)}) %all-to-all-start.6) | async-done | bytes 3145760 | tf_op jit(solution)/shard_map/all_to_all | solution.py:281
  537.1 10.6 all-to-all-start.3
  557.2 30.6 %all-to-all-done.3 = bf16[32,48,1024]{2,1,0:T(8,128)(2,1)} async-done(((bf16[32,48,1024]{2,1,0:T(8,128)(2,1)}), bf16[32,48,1024]{2,1,0:T(8,128)(2,1)}, u32[]{:S(2)}, u32[]{:S(2)}) %all-to-all-start.3) | async-done | bytes 3145760 | tf_op jit(solution)/shard_map/all_to_all | solution.py:219
  603.6 35.2 %all-to-all-done.7 = bf16[32,48,1024]{2,1,0:T(8,128)(2,1)} async-done(((bf16[32,48,1024]{2,1,0:T(8,128)(2,1)}), bf16[32,48,1024]{2,1,0:T(8,128)(2,1)}, u32[]{:S(2)}, u32[]{:S(2)}) %all-to-all-start.7) | async-done | bytes 3145760 | tf_op jit(solution)/shard_map/all_to_all | solution.py:256
  653.6 10.6 all-to-all-start.4
  671.2 33.6 %all-to-all-done.4 = bf16[32,48,1024]{2,1,0:T(8,128)(2,1)} async-done(((bf16[32,48,1024]{2,1,0:T(8,128)(2,1)}), bf16[32,48,1024]{2,1,0:T(8,128)(2,1)}, u32[]{:S(2)}, u32[]{:S(2)}) %all-to-all-start.4) | async-done | bytes 3145760 | tf_op jit(solution)/shard_map/all_to_all | solution.py:230
  729.2 26.6 %all-to-all-done.8 = bf16[32,48,1024]{2,1,0:T(8,128)(2,1)S(1)} async-done(((bf16[32,48,1024]{2,1,0:T(8,128)(2,1)}), bf16[32,48,1024]{2,1,0:T(8,128)(2,1)S(1)}, u32[]{:S(2)}, u32[]{:S(2)}) %all-to-all-start.8) | async-done | bytes 3145760 | tf_op jit(solution)/shard_map/all_to_all | solution.py:281
  829.0 116.0 %reduce-scatter.10.cloned.1.call-done = f32[32,512]{1,0:T(8,128)} async-done(((f32[1024,512]{1,0:T(8,128)}), f32[32,512]{1,0:T(8,128)}) %reduce-scatter.10.cloned.1.call-update) | async-done | bytes 65552 | tf_op jit(solution)/shard_map/reduce_scatter | solution.py:147
  945.0 184.9 %reduce-scatter.8.cloned.1.call-done = f32[32,512]{1,0:T(8,128)} async-done(((f32[1024,512]{1,0:T(8,128)}), f32[32,512]{1,0:T(8,128)}) %reduce-scatter.8.cloned.1.call-update) | async-done | bytes 65552 | tf_op jit(solution)/shard_map/reduce_scatter | solution.py:146
  1129.9 191.1 %reduce-scatter.12.cloned.1.call-done = f32[32,1024]{1,0:T(8,128)} async-done(((f32[1024,1024]{1,0:T(8,128)}), f32[32,1024]{1,0:T(8,128)}) %reduce-scatter.12.cloned.1.call-update) | async-done | bytes 131088 | tf_op jit(solution)/shard_map/reduce_scatter | solution.py:148
  1320.9 189.9 %reduce-scatter.6.cloned.1.call-done = f32[32,1024]{1,0:T(8,128)} async-done(((f32[1024,1024]{1,0:T(8,128)}), f32[32,1024]{1,0:T(8,128)}) %reduce-scatter.6.cloned.1.call-update) | async-done | bytes 131088 | tf_op jit(solution)/shard_map/reduce_scatter | solution.py:145
  1519.7 77.4 %all-reduce.4 = (f32[1024]{0:T(1024)S(1)}, f32[1024]{0:T(1024)S(1)}) all-reduce(f32[1024]{0:T(1024)S(1)} %add.332, f32[1024]{0:T(1024)S(1)} %copy-done.96), channel_id=9, replica_groups=mesh['rep'=4,'fsdp'=32] {'fsdp'}, use_global_device_ids=true, to_apply=%region_39.40.clone | all-reduce | flops 2048 | bytes 16384
  1600.5 89.2 %reduce-scatter.14.cloned.1.call-done = f32[32,32]{1,0:T(8,128)} async-done(((f32[1024,32]{1,0:T(8,128)}), f32[32,32]{1,0:T(8,128)}) %reduce-scatter.14.cloned.1.call-update) | async-done | bytes 4112 | tf_op jit(solution)/shard_map/reduce_scatter | solution.py:149
  1689.7 37.0 %all-reduce.5 = (f32[32]{0:T(128)}, f32[32]{0:T(128)}, f32[32,32]{1,0:T(8,128)}) all-reduce(f32[32]{0:T(128)S(1)} %dynamic-slice.3, f32[32]{0:T(128)S(1)} %dynamic-slice.5, f32[32,32]{1,0:T(8,128)} %reduce-scatter.14.cloned.1.call-done), channel_id=1, replica_groups=mesh['rep'=4,'fsdp'=32] {'rep'}, use_global_device_ids=true, to_apply=%region_42.43 | all-reduce | flops 1088 | bytes 8704 | tf_op jit(solution)/shard_map/psum | solution.py:347
  1726.7 120.2 %all-reduce.10.cloned.1.call-done = (f32[32,1024]{1,0:T(8,128)}, f32[32,512]{1,0:T(8,128)}, f32[32,512]{1,0:T(8,128)}, f32[32,1024]{1,0:T(8,128)}, f32[1,1024,51...) async-done(((f32[32,1024]{1,0:T(8,128)}, f32[32,512]{1,0:T(8,128)}, f32[32,512]{1,0:T(8,128)}, f32[32,1024]{1,0:T(8,128)}, f32[1,1024,512]{2,1,0:T(8,128)}, ...) | async-done | bytes 6684688 | tf_op jit(solution)/shard_map/psum | solution.py:347
  (479 shorter events, 336.5 us)
Async XLA Ops:
  7.2 389.9 %copy-start = (bf16[1,1024,512]{2,1,0:T(8,128)(2,1)S(1)}, bf16[1,1024,512]{2,1,0:T(8,128)(2,1)}, u32[]{:S(2)}) copy-start(bf16[1,1024,512]{2,1,0:T(8,128)(2,1)} %param.25) | copy-start | bytes 3145732
  7.2 116.2 %copy-start.103 = (s32[2,1,128]{2,1,0:T(1,128)S(1)}, s32[2,1,128]{2,1,0:T(1,128)}, u32[]{:S(2)}) copy-start(s32[2,1,128]{2,1,0:T(1,128)} %param.15) | copy-start | bytes 3076
  7.2 116.0 %copy-start.2 = (bf16[2,1,128,1024]{3,2,1,0:T(8,128)(2,1)S(1)}, bf16[2,1,128,1024]{3,2,1,0:T(8,128)(2,1)}, u32[]{:S(2)}) copy-start(bf16[2,1,128,1024]{3,2,1,0:T(8,128)(2,1)} %param.14) | copy-start | bytes 1572868
  7.2 117.5 %all-gather.5.cloned.1.call-start = ((), (), s32[]{:S(2)}) async-start(), calls=%async_computation.14 | async-start | bytes 1081344 | tf_op jit(solution)/shard_map/all_gather | solution.py:135
  8.0 137.5 %all-gather.7.cloned.1.call-start = ((), (), s32[]{:S(2)}) async-start(), calls=%async_computation.15 | async-start | bytes 1081344 | tf_op jit(solution)/shard_map/all_gather | solution.py:134
  8.7 208.2 %all-gather.9.cloned.1.call-start = ((), (), s32[]{:S(2)}) async-start(), calls=%async_computation.16 | async-start | bytes 2162688 | tf_op jit(solution)/shard_map/all_gather | solution.py:133
  11.0 287.0 %all-to-all-start = ((bf16[32,2,512]{2,1,0:T(2,128)(2,1)}), bf16[32,2,512]{2,1,0:T(2,128)(2,1)S(1)}, u32[]{:S(2)}, u32[]{:S(2)}) async-start(bf16[32,2,512]{2,1,0:T(2,128)(2,1)} %reshape.1095), calls=%async_computation | async-start | bytes 131072 | tf_op jit(solution)/shard_map/all_to_all | solution.py:23
  22.4 265.2 %all-gather.11.cloned.1.call-start = ((), (), s32[]{:S(2)}) async-start(), calls=%async_computation.17 | async-start | bytes 2162688 | tf_op jit(solution)/shard_map/all_gather | solution.py:136
  113.7 109.5 %copy-start.68 = (f32[128,64]{0,1:T(8,128)}, f32[128,64]{0,1:T(8,128)S(1)}, u32[]{:S(2)}) copy-start(f32[128,64]{0,1:T(8,128)S(1)} %get-tuple-element.115) | copy-start | bytes 98308
  124.0 166.7 %copy-start.94 = (s32[1024,1]{0,1:T(1,128)}, s32[1024,1]{0,1:T(1,128)S(1)}, u32[]{:S(2)}) copy-start(s32[1024,1]{0,1:T(1,128)S(1)} %compare_select_fusion.1) | copy-start | bytes 12292
  298.0 44.7 %all-to-all-start.1 = ((bf16[32,48,1024]{2,1,0:T(8,128)(2,1)}), bf16[32,48,1024]{2,1,0:T(8,128)(2,1)}, u32[]{:S(2)}, u32[]{:S(2)}) async-start(bf16[32,48,1024]{2,1,0:T(8,128)(2,1)} %bitcast.623), calls=%async_computation.1 | async-start | bytes 6291456 | tf_op jit(solution)/shard_map/all_to_all | solution.py:219
  342.7 50.1 %all-to-all-start.5 = ((bf16[32,48,1024]{2,1,0:T(8,128)(2,1)}), bf16[32,48,1024]{2,1,0:T(8,128)(2,1)}, u32[]{:S(2)}, u32[]{:S(2)}) async-start(bf16[32,48,1024]{2,1,0:T(8,128)(2,1)} %bitcast.625), calls=%async_computation.5 | async-start | bytes 6291456 | tf_op jit(solution)/shard_map/all_to_all | solution.py:256
  408.2 49.8 %all-to-all-start.2 = ((bf16[32,48,1024]{2,1,0:T(8,128)(2,1)}), bf16[32,48,1024]{2,1,0:T(8,128)(2,1)}, u32[]{:S(2)}, u32[]{:S(2)}) async-start(bf16[32,48,1024]{2,1,0:T(8,128)(2,1)} %convolution_convert_fusion.1), calls=%async_computation.2 | async-start | bytes 6291456 | tf_op jit(solution)/shard_map/all_to_all | solution.py:230
  458.0 59.6 %all-to-all-start.6 = ((bf16[32,48,1024]{2,1,0:T(8,128)(2,1)}), bf16[32,48,1024]{2,1,0:T(8,128)(2,1)}, u32[]{:S(2)}, u32[]{:S(2)}) async-start(bf16[32,48,1024]{2,1,0:T(8,128)(2,1)} %add_convert_fusion.1), calls=%async_computation.6 | async-start | bytes 6291456 | tf_op jit(solution)/shard_map/all_to_all | solution.py:281
  537.1 50.7 %all-to-all-start.3 = ((bf16[32,48,1024]{2,1,0:T(8,128)(2,1)}), bf16[32,48,1024]{2,1,0:T(8,128)(2,1)}, u32[]{:S(2)}, u32[]{:S(2)}) async-start(bf16[32,48,1024]{2,1,0:T(8,128)(2,1)} %bitcast.624), calls=%async_computation.3 | async-start | bytes 6291456 | tf_op jit(solution)/shard_map/all_to_all | solution.py:219
  587.8 50.9 %all-to-all-start.7 = ((bf16[32,48,1024]{2,1,0:T(8,128)(2,1)}), bf16[32,48,1024]{2,1,0:T(8,128)(2,1)}, u32[]{:S(2)}, u32[]{:S(2)}) async-start(bf16[32,48,1024]{2,1,0:T(8,128)(2,1)} %bitcast.626), calls=%async_computation.7 | async-start | bytes 6291456 | tf_op jit(solution)/shard_map/all_to_all | solution.py:256
  653.6 51.2 %all-to-all-start.4 = ((bf16[32,48,1024]{2,1,0:T(8,128)(2,1)}), bf16[32,48,1024]{2,1,0:T(8,128)(2,1)}, u32[]{:S(2)}, u32[]{:S(2)}) async-start(bf16[32,48,1024]{2,1,0:T(8,128)(2,1)} %convolution_convert_fusion), calls=%async_computation.4 | async-start | bytes 6291456 | tf_op jit(solution)/shard_map/all_to_all | solution.py:230
  704.8 51.0 %all-to-all-start.8 = ((bf16[32,48,1024]{2,1,0:T(8,128)(2,1)}), bf16[32,48,1024]{2,1,0:T(8,128)(2,1)S(1)}, u32[]{:S(2)}, u32[]{:S(2)}) async-start(bf16[32,48,1024]{2,1,0:T(8,128)(2,1)} %add_convert_fusion), calls=%async_computation.8 | async-start | bytes 6291456 | tf_op jit(solution)/shard_map/all_to_all | solution.py:281
  715.3 229.7 %reduce-scatter.10.cloned.1.call-start = ((), (), s32[]{:S(2)}) async-start(), calls=%async_computation.20 | async-start | bytes 2162688 | tf_op jit(solution)/shard_map/reduce_scatter | solution.py:147
  779.7 350.2 %reduce-scatter.8.cloned.1.call-start = ((), (), s32[]{:S(2)}) async-start(), calls=%async_computation.19 | async-start | bytes 2162688 | tf_op jit(solution)/shard_map/reduce_scatter | solution.py:146
  786.3 534.7 %reduce-scatter.12.cloned.1.call-start = ((), (), s32[]{:S(2)}) async-start(), calls=%async_computation.21 | async-start | bytes 4325376 | tf_op jit(solution)/shard_map/reduce_scatter | solution.py:148
  790.1 720.8 %reduce-scatter.6.cloned.1.call-start = ((), (), s32[]{:S(2)}) async-start(), calls=%async_computation.18 | async-start | bytes 4325376 | tf_op jit(solution)/shard_map/reduce_scatter | solution.py:145
  797.5 892.2 %reduce-scatter.14.cloned.1.call-start = ((), (), s32[]{:S(2)}) async-start(), calls=%async_computation.22 | async-start | bytes 540672 | tf_op jit(solution)/shard_map/reduce_scatter | solution.py:149
  822.5 1024.4 %all-reduce.10.cloned.1.call-start = ((), (), s32[]{:S(2)}) async-start(), calls=%async_computation.23 | async-start | bytes 13369344 | tf_op jit(solution)/shard_map/psum | solution.py:347
  (118 other events, 1567.2 us)
Sparse Core Ops, SparseCore 0:
  11.0 67.9 all-gather.4
  82.0 63.4 all-gather.6
  148.6 68.2 all-gather.8
  219.8 67.6 all-gather.10
  779.8 165.1 reduce-scatter.9
  947.9 181.9 reduce-scatter.7
  1132.3 188.6 reduce-scatter.11
  1323.3 187.4 reduce-scatter.5
  1513.2 176.4 reduce-scatter.13
  1693.5 153.3 all-reduce.9
